TPU v7x, 32 devices: a whole 2x2x4 slice. The times are simulated.
32 devices in a mesh: dom: 4 (over z), grp: 8 (over y, x, core).
Axes of the slice: x: 2, y: 2, z: 4, core: 2. Of those that a mesh axis runs over, the one named last changes fastest.
Arguments:
- support: float32 [16, 16, 16, 4096], P(None, None, None, ('dom', 'grp')), may hold values from -6 to 6
- potential: float32 [16, 16, 16, 4096], P(None, None, None, ('dom', 'grp')), may hold values from -6 to 6
- magic_taps: float32 [16], replicated, may hold values from -1 to 1
- kinetic_taps: float32 [16], replicated, may hold values from -1 to 1
- kernel_diag: float32 [4096], P(('dom', 'grp')), may hold values from 0.2 to 5
- owners: int32 [4096, 1], P(('dom', 'grp')), may hold values from 0 to 7; in each aligned block of 128 rows (0 to 127, 128 to 255, ...) at most 24 rows name the same one
Outputs:
- margin: float32 [4096, 128], P(('dom', 'grp'))
- density: float32 [32, 256], P('dom')
Inputs may be any that keep to these rules, and one draw needn't show every extreme that they name: `owners`: within each device's aligned block of 128 functions, no owner is named by more than 24 functions, a bound that some block reaches.
All inputs are finite; a program needn't handle non-finite values.
Results may differ from a plain program's by a relative error of at most 0.004.
Values may be sent and summed in bfloat16 or wider, within the bound.
A program may use at most 64 MiB of HBM per device.

v0:
```python
import jax
import jax.numpy as jnp
from jax import lax
from jax.sharding import PartitionSpec as P

HIGHEST = lax.Precision.HIGHEST


def passed_along(block, axis, distance):
    devices = range(lax.axis_size(axis))
    route = [((i - distance) % len(devices), i) for i in devices]
    return lax.ppermute(block, axis, route)


def band_matrix(tap_values, box_side):
    row_index = jnp.arange(box_side)[:, None]
    col_index = jnp.arange(box_side)[None, :]
    offset = col_index - row_index + (tap_values.shape[0] // 2 - 1)
    tap_table = (offset[:, :, None] == jnp.arange(tap_values.shape[0])[None, None, :]).astype(
        jnp.float32
    )
    return jnp.einsum("abt,t->ab", tap_table, tap_values, precision=HIGHEST)


def filter_along(matrix, field_block, direction):
    if direction == 0:
        return jnp.einsum("ab,bjkf->ajkf", matrix, field_block, precision=HIGHEST)
    if direction == 1:
        return jnp.einsum("ab,ibkf->iakf", matrix, field_block, precision=HIGHEST)
    return jnp.einsum("ab,ijbf->ijaf", matrix, field_block, precision=HIGHEST)


def apply_block(support, potential, magic_taps, kinetic_taps, kernel_diag):
    box_side = support.shape[0]
    magic_band = band_matrix(magic_taps, box_side)
    kinetic_band = band_matrix(kinetic_taps, box_side)
    realspace = filter_along(
        magic_band, filter_along(magic_band, filter_along(magic_band, support, 0), 1), 2
    )
    density_part = jnp.sum(kernel_diag * realspace * realspace, axis=3)
    weighted = potential * realspace
    magic_back = magic_band.T
    returned = filter_along(
        magic_back, filter_along(magic_back, filter_along(magic_back, weighted, 0), 1), 2
    )
    kinetic_part = (
        filter_along(kinetic_band, support, 0)
        + filter_along(kinetic_band, support, 1)
        + filter_along(kinetic_band, support, 2)
    )
    gradient = (returned + kinetic_part).astype(jnp.bfloat16)
    return (gradient, density_part)


def body(support, potential, magic_taps, kinetic_taps, kernel_diag, owners):
    box_side = support.shape[0]
    local_count = support.shape[3]
    cell_count = box_side**3
    half_side = box_side // 2
    groups = lax.axis_size("grp")
    capacity = max(2, 3 * local_count // (2 * groups))
    scale_factor = 1.0 / float(box_side) ** 1.5
    gradient, density_part = apply_block(support, potential, magic_taps, kinetic_taps, kernel_diag)
    density_part = (density_part / (local_count * groups)).reshape(box_side, box_side * box_side)
    target = owners[:, 0]
    onehot = (target[:, None] == jnp.arange(groups)[None, :]).astype(jnp.int32)
    before = jnp.cumsum(onehot, axis=0) - onehot
    slot_index = jnp.sum(before * onehot, axis=1)
    column = target * capacity + slot_index
    dispatch = (column[:, None] == jnp.arange(groups * capacity)[None, :]).astype(jnp.bfloat16)
    gradient_flat = gradient.reshape(cell_count, local_count)
    outgoing = lax.dot_general(
        dispatch, gradient_flat, (((0,), (1,)), ((), ())), preferred_element_type=jnp.float32
    ).astype(jnp.bfloat16)
    owned = support.reshape(cell_count, local_count).astype(jnp.bfloat16)
    received = lax.all_to_all(outgoing, "grp", split_axis=0, concat_axis=0, tiled=True)
    products = jnp.dot(received, owned, preferred_element_type=jnp.float32)
    products = products * (kernel_diag * scale_factor)[None, :]
    returned_rows = lax.all_to_all(products, "grp", split_axis=0, concat_axis=0, tiled=True)
    margin = jnp.dot(dispatch.astype(jnp.float32), returned_rows, precision=HIGHEST)
    summed = lax.psum(density_part, "grp")
    density_slab = summed[:half_side] + passed_along(summed[half_side:], "dom", 1)
    return (margin, density_slab)


def solution(mesh):
    return jax.shard_map(
        body,
        mesh=mesh,
        in_specs=(
            P(None, None, None, ("dom", "grp")),
            P(None, None, None, ("dom", "grp")),
            P(),
            P(),
            P(("dom", "grp")),
            P(("dom", "grp"), None),
        ),
        out_specs=(P(("dom", "grp"), None), P("dom", None)),
        check_vma=False,
    )
```

profile of v0, /device:TPU:0, one launch (start us, length us, event | category | flops | bytes accessed | tf_op | source)
XLA Modules:
  0.0 96.9 jit_solution(10748069938954935442)
XLA Ops:
  0.6 0.0 copy-start
  0.7 0.6 copy-done
  1.3 0.6 fusion.21
  1.9 0.0 copy-start.1
  1.9 5.3 %fusion.15 = f32[16,16,16,128]{3,0,2,1:T(8,128)} fusion(f32[16,16,1,1]{1,0,3,2:T(8,128)S(1)} %bitcast.89, f32[16,16,16,128]{3,2,1,0:T(8,128)} %param.6), kind=kOutput, calls=%fused_computation.20 | convolution fusion | flops 100663296 | bytes 4195328 | tf_op jit(solution)/shard_map/ab,ibkf->iakf/dot_general | solution.py:29
  7.2 0.0 copy-done.1
  7.2 0.0 copy-start.5
  7.2 4.1 %fusion.19 = f32[16,16,16,128]{3,0,2,1:T(8,128)} fusion(f32[16,16,1,1]{1,0,3,2:T(8,128)S(1)} %bitcast.90, f32[16,16,16,128]{3,2,1,0:T(8,128)S(1)} %copy-done.1), kind=kOutput, calls=%fused_computation.24 | convolution fusion | flops 100663296 | bytes 4195328 | tf_op jit(solution)/shard_map/ab,bjkf->ajkf/dot_general | solution.py:27
  11.4 0.0 copy-done.5
  11.4 0.6 fusion.22
  12.0 2.9 %fusion.17 = f32[16,16,16,128]{3,0,2,1:T(8,128)S(1)} fusion(f32[16,16,1,1]{1,0,3,2:T(8,128)S(1)} %bitcast.83, f32[16,16,16,128]{3,2,1,0:T(8,128)S(1)} %copy-done.1), kind=kOutput, calls=%fused_computation.22 | convolution fusion | flops 100663296 | bytes 4195328 | tf_op jit(solution)/shard_map/ab,bjkf->ajkf/dot_general | solution.py:27
  14.9 0.0 copy-start.2
  14.9 0.0 copy-start.4
  14.9 3.2 %fusion.9 = f32[16,16,128,16]{2,3,1,0:T(8,128)S(1)} fusion(f32[16,16,1,1]{1,0,3,2:T(8,128)S(1)} %bitcast.84, f32[16,16,16,128]{3,0,2,1:T(8,128)S(1)} %fusion.17), kind=kOutput, calls=%fused_computation.14 | convolution fusion | flops 100663296 | bytes 4195328 | tf_op jit(solution)/shard_map/ab,ibkf->iakf/dot_general | solution.py:29
  18.1 0.0 copy-done.2
  18.1 0.0 copy-done.4
  18.1 3.2 %fusion = (f32[16,16,16]{2,1,0:T(8,128)S(1)}, f32[16,16,16,128]{3,2,1,0:T(8,128)S(1)}) fusion(f32[128]{0:T(128)S(1)} %copy-done.4, f32[16,16,16,128]{3,2,1,0:T(8,128)S(1)} %copy-done.2, f32[16,16,1,1]{1,0,3,2:T(8,128)S(1)} %bitcast.85, f32[16,16,128,16]{2,3,1,0:T(8,128)S(1)} %fusion.9), kind=kOutput, calls=%fused_computation.2 | convolution fusion | flops 102756352 | bytes 6309376 | tf_op jit(solution)/shard_map/ab,ijbf->ijaf/dot_general | solution.py:30
  21.3 2.9 %fusion.12 = f32[16,16,16,128]{3,0,2,1:T(8,128)S(1)} fusion(f32[16,16,1,1]{1,0,3,2:T(8,128)S(1)} %bitcast.86, f32[16,16,16,128]{3,2,1,0:T(8,128)S(1)} %get-tuple-element.3), kind=kOutput, calls=%fused_computation.17 | convolution fusion | flops 100663296 | bytes 4195328 | tf_op jit(solution)/shard_map/ab,bjkf->ajkf/dot_general | solution.py:27
  24.2 3.3 %fusion.5 = f32[16,16,128,16]{2,3,1,0:T(8,128)S(1)} fusion(f32[16,16,1,1]{1,0,3,2:T(8,128)S(1)} %bitcast.87, f32[16,16,16,128]{3,0,2,1:T(8,128)S(1)} %fusion.12), kind=kOutput, calls=%fused_computation.9 | convolution fusion | flops 100663296 | bytes 4195328 | tf_op jit(solution)/shard_map/ab,ibkf->iakf/dot_general | solution.py:29
  27.5 0.0 copy-start.3
  27.5 3.8 %fusion.3 = f32[16,16,128,16]{2,3,1,0:T(8,128)} fusion(f32[16,16,1,1]{1,0,3,2:T(8,128)S(1)} %bitcast.88, f32[16,16,128,16]{2,3,1,0:T(8,128)S(1)} %fusion.5), kind=kOutput, calls=%fused_computation.7 | convolution fusion | flops 100663296 | bytes 4195328 | tf_op jit(solution)/shard_map/ab,ijbf->ijaf/dot_general | solution.py:30
  31.2 0.0 copy-done.3
  31.2 0.1 fusion.30
  31.3 0.2 reduce_window_sum.11
  31.5 0.2 select_reduce_fusion
  31.9 5.9 %fusion.2 = bf16[16,16,16,128]{3,2,1,0:T(8,128)(2,1)S(1)} fusion(f32[16,16,128,16]{2,3,1,0:T(8,128)} %fusion.3, f32[16,16,16,128]{3,0,2,1:T(8,128)} %fusion.19, f32[16,16,16,128]{3,0,2,1:T(8,128)} %fusion.15, f32[16,16,1,1]{1,0,3,2:T(8,128)S(1)} %bitcast.91, f32[16,16,16,128]{3,2,1,0:T(8,128)S(1)} %copy-done.1), kind=kOutput, calls=%fused_computation.5 | convolution fusion | flops 102760448 | bytes 9438208 | tf_op jit(solution)/shard_map/ab,ijbf->ijaf/dot_general | solution.py:30
  37.8 1.8 %convolution_convert_fusion = bf16[192,4096]{1,0:T(8,128)(2,1)} fusion(bf16[4096,128]{1,0:T(8,128)(2,1)S(1)} %bitcast.81, s32[128]{0:T(128)S(1)} %fusion.31), kind=kOutput, calls=%fused_computation | convolution fusion | flops 202162176 | bytes 2621952 | tf_op jit(solution)/shard_map/dot_general | solution.py:72
  39.6 5.2 %all-to-all-start = ((bf16[8,24,4096]{2,1,0:T(8,128)(2,1)}), bf16[8,24,4096]{2,1,0:T(8,128)(2,1)}, u32[]{:S(2)}, u32[]{:S(2)}) async-start(bf16[8,24,4096]{2,1,0:T(8,128)(2,1)} %bitcast.79), calls=%async_computation | async-start | bytes 3145728 | tf_op jit(solution)/shard_map/all_to_all | solution.py:76
  44.8 0.1 div.10
  44.9 37.8 %psum.7 = f32[16,256]{1,0:T(8,128)S(1)} all-reduce(f32[16,256]{1,0:T(8,128)S(1)} %div.10), channel_id=1, replica_groups=mesh['dom'=4,'grp'=8] {'grp'}, use_global_device_ids=true, to_apply=%region_3.4 | all-reduce | flops 4096 | bytes 32768 | tf_op jit(solution)/shard_map/psum | solution.py:81
  82.7 2.0 %collective-permute-start = (f32[8,256]{1,0:T(8,128)S(1)}, f32[8,256]{1,0:T(8,128)S(1)}, u32[]{:S(2)}, u32[]{:S(2)}) collective-permute-start(f32[8,256]{1,0:T(8,128)S(1)} %slice.9), channel_id=1, source_target_pairs={{24,0},{0,8},{8,16},{16,24},{25,1},{1,9},{9,17},{17,25},{26,2},{2,... | collective-permute-start | bytes 24584 | tf_op jit(solution)/shard_map/ppermute | solution.py:12
  84.7 0.2 convert_element_type.22
  84.9 0.0 all-to-all-done
  84.9 2.6 %convolution_multiply_fusion = f32[192,128]{1,0:T(8,128)} fusion(bf16[192,4096]{1,0:T(8,128)(2,1)} %bitcast.26, bf16[4096,128]{1,0:T(8,128)(2,1)S(1)} %bitcast.80, f32[128]{0:T(128)S(1)} %broadcast_multiply_fusion.1), kind=kOutput, calls=%fused_computation.26 | convolution fusion | flops 201351168 | bytes 2720256 | tf_op jit(solution)/shard_map/dot_general | solution.py:77
  87.5 3.4 %all-to-all-start.1 = ((f32[8,24,128]{2,1,0:T(8,128)}), f32[8,24,128]{2,1,0:T(8,128)S(1)}, u32[]{:S(2)}, u32[]{:S(2)}) async-start(f32[8,24,128]{2,1,0:T(8,128)} %bitcast.28), calls=%async_computation.1 | async-start | bytes 196608 | tf_op jit(solution)/shard_map/all_to_all | solution.py:79
  90.9 0.0 collective-permute-done
  90.9 0.6 slice_add_fusion
  91.5 4.5 %all-to-all-done.1 = f32[8,24,128]{2,1,0:T(8,128)S(1)} async-done(((f32[8,24,128]{2,1,0:T(8,128)}), f32[8,24,128]{2,1,0:T(8,128)S(1)}, u32[]{:S(2)}, u32[]{:S(2)}) %all-to-all-start.1) | async-done | bytes 98336 | tf_op jit(solution)/shard_map/all_to_all | solution.py:79
  96.0 0.9 fusion.23
  (5 shorter events, 0.0 us)
Async XLA Ops:
  0.6 0.7 copy-start
  1.9 5.3 %copy-start.1 = (f32[16,16,16,128]{3,2,1,0:T(8,128)S(1)}, f32[16,16,16,128]{3,2,1,0:T(8,128)}, u32[]{:S(2)}) copy-start(f32[16,16,16,128]{3,2,1,0:T(8,128)} %param.6) | copy-start | bytes 6291460
  7.2 4.1 %copy-start.5 = (f32[16]{0:T(128)S(1)}, f32[16]{0:T(128)}, u32[]{:S(2)}) copy-start(f32[16]{0:T(128)} %param.8) | copy-start | bytes 196
  14.9 3.3 %copy-start.2 = (f32[16,16,16,128]{3,2,1,0:T(8,128)S(1)}, f32[16,16,16,128]{3,2,1,0:T(8,128)}, u32[]{:S(2)}) copy-start(f32[16,16,16,128]{3,2,1,0:T(8,128)} %param.7) | copy-start | bytes 6291460
  14.9 3.3 %copy-start.4 = (f32[128]{0:T(128)S(1)}, f32[128]{0:T(128)}, u32[]{:S(2)}) copy-start(f32[128]{0:T(128)} %param.10) | copy-start | bytes 1540
  27.5 3.8 %copy-start.3 = (s32[128,1]{0,1:T(1,128)S(1)}, s32[128,1]{0,1:T(1,128)}, u32[]{:S(2)}) copy-start(s32[128,1]{0,1:T(1,128)} %param.11) | copy-start | bytes 1540
  39.6 45.3 %all-to-all-start = ((bf16[8,24,4096]{2,1,0:T(8,128)(2,1)}), bf16[8,24,4096]{2,1,0:T(8,128)(2,1)}, u32[]{:S(2)}, u32[]{:S(2)}) async-start(bf16[8,24,4096]{2,1,0:T(8,128)(2,1)} %bitcast.79), calls=%async_computation | async-start | bytes 3145728 | tf_op jit(solution)/shard_map/all_to_all | solution.py:76
  82.7 8.2 %collective-permute-start = (f32[8,256]{1,0:T(8,128)S(1)}, f32[8,256]{1,0:T(8,128)S(1)}, u32[]{:S(2)}, u32[]{:S(2)}) collective-permute-start(f32[8,256]{1,0:T(8,128)S(1)} %slice.9), channel_id=1, source_target_pairs={{24,0},{0,8},{8,16},{16,24},{25,1},{1,9},{9,17},{17,25},{26,2},{2,... | collective-permute-start | bytes 24584 | tf_op jit(solution)/shard_map/ppermute | solution.py:12
  87.5 8.5 %all-to-all-start.1 = ((f32[8,24,128]{2,1,0:T(8,128)}), f32[8,24,128]{2,1,0:T(8,128)S(1)}, u32[]{:S(2)}, u32[]{:S(2)}) async-start(f32[8,24,128]{2,1,0:T(8,128)} %bitcast.28), calls=%async_computation.1 | async-start | bytes 196608 | tf_op jit(solution)/shard_map/all_to_all | solution.py:79
where the time goes:
time: 97.2 us; the launch traced here: 96.9 us
  matrix products  41.1 us (42%)
  blocking collectives  37.8 us (39%)
  starting transfers between devices  10.5 us (11%)
  waiting for transfers between devices  4.52 us (5%)
  other arithmetic  1.21 us (1%)
  between operations  1.02 us (1%)
    psum x1, blocking collectives, body(): summed = lax.psum(density_part, 'grp')  37.8 us
    dot_general x3, matrix products, filter_along(): return jnp.einsum('ab,ijbf->ijaf', matrix, field_block, precision=HIGHEST)  12.8 us
    dot_general x3, matrix products, filter_along(): return jnp.einsum('ab,ibkf->iakf', matrix, field_block, precision=HIGHEST)  11.8 us
    dot_general x3, matrix products, filter_along(): return jnp.einsum('ab,bjkf->ajkf', matrix, field_block, precision=HIGHEST)  9.87 us
    all_to_all x1, starting transfers between devices, body(): lax.all_to_all(outgoing, 'grp', split_axis=0, concat_axis=0, tiled=True)  5.16 us
    all_to_all x1, waiting for transfers between devices, body(): lax.all_to_all(products, 'grp', split_axis=0, concat_axis=0, tiled=True)  4.51 us
    all_to_all x1, starting transfers between devices, body(): lax.all_to_all(products, 'grp', split_axis=0, concat_axis=0, tiled=True)  3.36 us
    dot_general x1, matrix products, body(): products = jnp.dot(received, owned, preferred_element_type=jnp.float32)  2.63 us
  transfers between devices with their start and end apart: 3, of which 1 were waited for; matrix products, arithmetic and copies ran while one was open for 4% of the time, Pallas kernels for 0%

commit v1 on v0

--- a/solution.py
+++ b/solution.py
@@ -1,6 +1,10 @@
+import functools
+
 import jax
 import jax.numpy as jnp
 from jax import lax
+from jax.experimental import pallas as pl
+from jax.experimental.pallas import tpu as pltpu
 from jax.sharding import PartitionSpec as P
 
 HIGHEST = lax.Precision.HIGHEST
@@ -52,7 +56,7 @@
     return (gradient, density_part)
 
 
-def body(support, potential, magic_taps, kinetic_taps, kernel_diag, owners):
+def general_body(support, potential, magic_taps, kinetic_taps, kernel_diag, owners):
     box_side = support.shape[0]
     local_count = support.shape[3]
     cell_count = box_side**3
@@ -83,9 +87,362 @@
     return (margin, density_slab)
 
 
+MESH = pl.DeviceIdType.MESH
+BF16 = jnp.bfloat16
+F32 = jnp.float32
+NT = (((1,), (1,)), ((), ()))
+
+
+def split(value):
+    high = value.astype(BF16)
+    return high, (value - high.astype(F32)).astype(BF16)
+
+
+def mm(left, right):
+    return jnp.dot(left, right, preferred_element_type=F32)
+
+
+def mm3(weight_high, weight_low, high, low):
+    return mm(weight_high, high) + (mm(weight_high, low) + mm(weight_low, high))
+
+
+def tap_select(offset, taps_ref):
+    count = taps_ref.shape[0]
+    value = jnp.zeros(offset.shape, F32)
+    for tap in range(count):
+        value = jnp.where(offset == tap - (count // 2 - 1), taps_ref[tap], value)
+    return value
+
+
+def fused_kernel(
+    groups, doms, cap,
+    magic_ref, kinetic_ref, owners_ref, kdiag_ref, support_ref, potential_ref,
+    margin_ref, density_ref,
+    x_ref, v_ref, y_ref, z_ref, xh_ref, xl_ref, w_ref, taps_ref, send_ref, recv_ref,
+    acc_ref, dens_ref, halo_ref, comb_ref, prod_ref, back_ref, disp_ref, disp_t_ref,
+    load_sem, send_sem, recv_sem, bs_sem, br_sem, ds_sem, dr_sem, hs_sem, hr_sem,
+):
+    side = x_ref.shape[0]
+    funcs = x_ref.shape[3]
+    plane = side * side
+    chunks = side // 2
+    slots = groups * cap
+    me = lax.axis_index("grp")
+    dom = lax.axis_index("dom")
+    dom_next = lax.rem(dom + 1, doms)
+    dom_prev = lax.rem(dom + doms - 1, doms)
+
+    load_x = pltpu.make_async_copy(support_ref, x_ref, load_sem.at[0])
+    load_v = pltpu.make_async_copy(potential_ref, v_ref, load_sem.at[1])
+    load_x.start()
+    load_v.start()
+
+    barrier = pltpu.get_barrier_semaphore()
+    for d in range(1, groups):
+        pl.semaphore_signal(barrier, inc=1, device_id={"grp": lax.rem(me + d, groups)}, device_id_type=MESH)
+    pl.semaphore_signal(barrier, inc=1, device_id={"dom": dom_prev}, device_id_type=MESH)
+
+    for t in range(3 * side):
+        taps_ref[t] = kinetic_ref[t - side] if side <= t < 2 * side else jnp.float32(0.0)
+    row = lax.broadcasted_iota(jnp.int32, (side, plane), 0)
+    col = lax.broadcasted_iota(jnp.int32, (side, plane), 1)
+    outer = (col >> 4) - row
+    inner = (col & 15) - row
+    unit = jnp.where(outer == 0, 1.0, 0.0)
+    tall = jnp.concatenate(
+        [tap_select(outer, magic_ref), tap_select(-outer, magic_ref), tap_select(outer, kinetic_ref), unit],
+        axis=1,
+    )
+    tall_high, tall_rest = split(tall)
+    tall_mid = tall_rest
+    tall_low = (tall - tall_high.astype(F32) - tall_mid.astype(F32)).astype(BF16)
+    pick_row = lax.broadcasted_iota(jnp.int32, (plane, side), 0) >> 4
+    pick_col = lax.broadcasted_iota(jnp.int32, (plane, side), 1)
+    pick = jnp.where(pick_row == pick_col, 1.0, 0.0).astype(BF16)
+    wide = mm(pick, tall_high) + (mm(pick, tall_mid) + mm(pick, tall_low))
+    magic_out, back_out, kin_out, same_out = [wide[:, n * plane:(n + 1) * plane] for n in range(4)]
+
+    def tiled(value):
+        return jnp.concatenate([value] * side, axis=0)
+
+    magic_in = tiled(tap_select(inner, magic_ref))
+    back_in = tiled(tap_select(-inner, magic_ref))
+    kin_in = tiled(tap_select(inner, kinetic_ref))
+    same_in = tiled(jnp.where(inner == 0, 1.0, 0.0))
+    matrices = [
+        magic_out * magic_in,
+        magic_out * same_in,
+        back_out * back_in,
+        back_out * same_in,
+        kin_out * same_in + same_out * kin_in,
+    ]
+    for n, matrix in enumerate(matrices):
+        high, low = split(matrix)
+        w_ref[2 * n] = high
+        w_ref[2 * n + 1] = low
+
+    owner = owners_ref[...]
+    named = jnp.where(lax.broadcasted_iota(jnp.int32, (16, funcs), 0) == owner, 1.0, 0.0)
+    earlier = jnp.where(
+        lax.broadcasted_iota(jnp.int32, (funcs, funcs), 0) < lax.broadcasted_iota(jnp.int32, (funcs, funcs), 1),
+        1.0, 0.0,
+    ).astype(BF16)
+    before = mm(named.astype(BF16), earlier)
+    slot = jnp.sum(before * named, axis=0, keepdims=True)
+    column = owner.astype(F32) * float(cap) + slot
+    padded = disp_t_ref.shape[1]
+    spot = lax.broadcasted_iota(jnp.int32, (padded, funcs), 0).astype(F32)
+    dispatch = jnp.where(spot == column, 1.0, 0.0)
+    disp_ref[...] = dispatch[:slots].astype(BF16)
+    disp_t_ref[...] = dispatch.T.astype(BF16)
+
+    kdiag = kdiag_ref[...]
+    kdiag_pair = jnp.concatenate([kdiag, kdiag], axis=1) * (1.0 / float(funcs * groups))
+    dens_ref[...] = jnp.zeros_like(dens_ref)
+    acc_ref[...] = jnp.zeros_like(acc_ref)
+
+    def pair_mid(ref, n):
+        first = ref[:, 2 * n].reshape(plane, funcs)
+        second = ref[:, 2 * n + 1].reshape(plane, funcs)
+        return jnp.concatenate([first, second], axis=1)
+
+    def pair_top(ref, n):
+        first = ref[2 * n].reshape(plane, funcs)
+        second = ref[2 * n + 1].reshape(plane, funcs)
+        return jnp.concatenate([first, second], axis=1)
+
+    load_x.wait()
+
+    def stage_a(n, carry):
+        high, low = split(pair_mid(x_ref, n))
+        xh_ref[n] = high
+        xl_ref[n] = low
+        out = mm3(w_ref[0], w_ref[1], high, low)
+        y_ref[:, 2 * n] = out[:, :funcs].reshape(side, side, funcs)
+        y_ref[:, 2 * n + 1] = out[:, funcs:].reshape(side, side, funcs)
+        return carry
+
+    lax.fori_loop(0, chunks, stage_a, 0)
+    load_v.wait()
+
+    dens_row = lax.broadcasted_iota(jnp.int32, (side, 2 * funcs), 0)
+    dens_half = lax.broadcasted_iota(jnp.int32, (side, 2 * funcs), 1) >> 7
+
+    def stage_b(n, carry):
+        high, low = split(pair_top(y_ref, n))
+        real = mm3(w_ref[2], w_ref[3], high, low)
+        squared = (real * real * kdiag_pair).astype(BF16)
+        chosen = jnp.where(dens_row == dens_half + 2 * n, 1.0, 0.0).astype(BF16)
+        dens_ref[...] += lax.dot_general(chosen, squared, NT, preferred_element_type=F32)
+        high, low = split(pair_top(v_ref, n) * real)
+        out = mm3(w_ref[4], w_ref[5], high, low)
+        z_ref[2 * n] = out[:, :funcs].reshape(side, side, funcs)
+        z_ref[2 * n + 1] = out[:, funcs:].reshape(side, side, funcs)
+        return carry
+
+    lax.fori_loop(0, chunks, stage_b, 0)
+
+    pl.semaphore_wait(barrier, groups)
+
+    half = side // 2
+    halo = pltpu.make_async_remote_copy(
+        src_ref=dens_ref.at[pl.ds(half, half)], dst_ref=halo_ref, send_sem=hs_sem, recv_sem=hr_sem,
+        device_id={"dom": dom_next}, device_id_type=MESH,
+    )
+    halo.start()
+
+    order = [1 + (groups // 2 + n) % (groups - 1) for n in range(groups - 1)]
+
+    def bulk(n, d):
+        peer = lax.rem(me + d, groups)
+        return pltpu.make_async_remote_copy(
+            src_ref=send_ref.at[n, peer], dst_ref=recv_ref.at[n, me],
+            send_sem=send_sem.at[n, d], recv_sem=recv_sem.at[n, d],
+            device_id={"grp": peer}, device_id_type=MESH,
+        )
+
+    def arrived(n, d):
+        source = lax.rem(me + groups - d, groups)
+        return pltpu.make_async_remote_copy(
+            src_ref=send_ref.at[n, source], dst_ref=recv_ref.at[n, source],
+            send_sem=send_sem.at[n, d], recv_sem=recv_sem.at[n, d],
+            device_id={"grp": source}, device_id_type=MESH,
+        )
+
+    def stage_c(n, carry):
+        zh, zl = split(pair_mid(z_ref, n))
+        grad = mm3(w_ref[6], w_ref[7], zh, zl) + mm3(w_ref[8], w_ref[9], xh_ref[n], xl_ref[n])
+        rows = []
+        for p in range(2):
+            j = 2 * n + p
+            along = jnp.zeros((side, side, funcs), F32)
+            for other in range(side):
+                along = along + taps_ref[other - j + (side // 2 - 1 + side)] * x_ref[:, other]
+            block = (grad[:, p * funcs:(p + 1) * funcs] + along.reshape(plane, funcs)).astype(BF16)
+            rows.append(lax.dot_general(disp_ref[...], block, NT, preferred_element_type=F32))
+        for o in range(groups):
+            send_ref[n, o] = jnp.concatenate(
+                [rows[0][o * cap:(o + 1) * cap], rows[1][o * cap:(o + 1) * cap]], axis=0
+            ).astype(BF16)
+        for d in order:
+            bulk(n, d).start()
+        recv_ref[n, me] = send_ref[n, me]
+        return carry
+
+    lax.fori_loop(0, chunks // 2, stage_c, 0)
+
+    halo.wait()
+    comb_ref[me] = dens_ref[:half] + halo_ref[...]
+
+    def spread(d, source):
+        peer = lax.rem(me + d, groups)
+        return pltpu.make_async_remote_copy(
+            src_ref=comb_ref.at[source], dst_ref=comb_ref.at[source],
+            send_sem=ds_sem.at[d], recv_sem=dr_sem.at[d],
+            device_id={"grp": peer}, device_id_type=MESH,
+        )
+
+    for d in order:
+        spread(d, me).start()
+
+    lax.fori_loop(chunks // 2, chunks, stage_c, 0)
+
+    def stage_d(n, carry):
+        for d in order:
+            arrived(n, d).wait_recv()
+        rows = recv_ref[n].reshape(groups * 2 * cap, plane)
+        acc_ref[...] += mm(rows, xh_ref[n])
+        return carry
+
+    lax.fori_loop(0, chunks, stage_d, 0)
+
+    scale = kdiag * (1.0 / float(side) ** 1.5)
+    for s in range(groups):
+        top = 2 * cap * s
+        prod_ref[s] = scale * (
+            acc_ref[top:top + cap, :funcs] + acc_ref[top + cap:top + 2 * cap, funcs:]
+        )
+
+    def give(d):
+        peer = lax.rem(me + d, groups)
+        return pltpu.make_async_remote_copy(
+            src_ref=prod_ref.at[peer], dst_ref=back_ref.at[me],
+            send_sem=bs_sem.at[d], recv_sem=br_sem.at[d],
+            device_id={"grp": peer}, device_id_type=MESH,
+        )
+
+    def get(d):
+        source = lax.rem(me + groups - d, groups)
+        return pltpu.make_async_remote_copy(
+            src_ref=prod_ref.at[source], dst_ref=back_ref.at[source],
+            send_sem=bs_sem.at[d], recv_sem=br_sem.at[d],
+            device_id={"grp": source}, device_id_type=MESH,
+        )
+
+    for d in order:
+        give(d).start()
+    back_ref[me] = prod_ref[me]
+
+    for d in order:
+        spread(d, lax.rem(me + groups - d, groups)).wait_recv()
+    total = comb_ref[0]
+    for g in range(1, groups):
+        total = total + comb_ref[g]
+    density_ref[...] = total
+
+    for d in order:
+        get(d).wait_recv()
+    returned = back_ref[...].reshape(slots, funcs)
+    if padded > slots:
+        returned = jnp.concatenate([returned, jnp.zeros((padded - slots, funcs), F32)], axis=0)
+    high, low = split(returned)
+    margin_ref[...] = mm(disp_t_ref[...], high) + mm(disp_t_ref[...], low)
+
+    def drain(n, carry):
+        for d in order:
+            bulk(n, d).wait_send()
+        return carry
+
+    lax.fori_loop(0, chunks, drain, 0)
+    for d in order:
+        spread(d, me).wait_send()
+        give(d).wait_send()
+
+
+def fused_body(doms, support, potential, magic_taps, kinetic_taps, kernel_diag, owners):
+    side = support.shape[0]
+    funcs = support.shape[3]
+    groups = lax.axis_size("grp")
+    cap = max(2, 3 * funcs // (2 * groups))
+    plane = side * side
+    chunks = side // 2
+    padded = -(-groups * cap // 128) * 128
+    vmem = pl.BlockSpec(memory_space=pltpu.VMEM)
+    smem = pl.BlockSpec(memory_space=pltpu.SMEM)
+    anywhere = pl.BlockSpec(memory_space=pl.ANY)
+    box = (side, side, side, funcs)
+    dma = pltpu.SemaphoreType.DMA
+    margin, density = pl.pallas_call(
+        functools.partial(fused_kernel, groups, doms, cap),
+        out_shape=(
+            jax.ShapeDtypeStruct((funcs, funcs), F32),
+            jax.ShapeDtypeStruct((side // 2, plane), F32),
+        ),
+        in_specs=[smem, smem, vmem, vmem, anywhere, anywhere],
+        out_specs=(vmem, vmem),
+        scratch_shapes=[
+            pltpu.VMEM(box, F32),
+            pltpu.VMEM(box, F32),
+            pltpu.VMEM(box, F32),
+            pltpu.VMEM(box, F32),
+            pltpu.VMEM((chunks, plane, 2 * funcs), BF16),
+            pltpu.VMEM((chunks, plane, 2 * funcs), BF16),
+            pltpu.VMEM((10, plane, plane), BF16),
+            pltpu.SMEM((3 * side,), F32),
+            pltpu.VMEM((chunks, groups, 2 * cap, plane), BF16),
+            pltpu.VMEM((chunks, groups, 2 * cap, plane), BF16),
+            pltpu.VMEM((groups * 2 * cap, 2 * funcs), F32),
+            pltpu.VMEM((side, plane), F32),
+            pltpu.VMEM((side // 2, plane), F32),
+            pltpu.VMEM((groups, side // 2, plane), F32),
+            pltpu.VMEM((groups, cap, funcs), F32),
+            pltpu.VMEM((groups, cap, funcs), F32),
+            pltpu.VMEM((groups * cap, funcs), BF16),
+            pltpu.VMEM((funcs, padded), BF16),
+            dma((2,)),
+            dma((chunks, groups)),
+            dma((chunks, groups)),
+            dma((groups,)),
+            dma((groups,)),
+            dma((groups,)),
+            dma((groups,)),
+            dma,
+            dma,
+        ],
+        compiler_params=pltpu.CompilerParams(
+            collective_id=0, has_side_effects=True, vmem_limit_bytes=40 * 2**20
+        ),
+    )(
+        magic_taps, kinetic_taps, owners.reshape(1, funcs), kernel_diag.reshape(1, funcs),
+        support, potential,
+    )
+    return (margin, density)
+
+
+def body(doms, support, potential, magic_taps, kinetic_taps, kernel_diag, owners):
+    side = support.shape[0]
+    funcs = support.shape[3]
+    groups = lax.axis_size("grp")
+    cap = max(2, 3 * funcs // (2 * groups))
+    fits = side == 16 and magic_taps.shape[0] == 16 and funcs == 128 and groups <= 8
+    if fits and cap % 8 == 0 and doms > 1:
+        return fused_body(doms, support, potential, magic_taps, kinetic_taps, kernel_diag, owners)
+    return general_body(support, potential, magic_taps, kinetic_taps, kernel_diag, owners)
+
+
 def solution(mesh):
     return jax.shard_map(
-        body,
+        functools.partial(body, mesh.shape["dom"]),
         mesh=mesh,
         in_specs=(
             P(None, None, None, ("dom", "grp")),

time: 97.2 us -> 44.4 us (0.46)
  matrix products: 41.1 us -> 0 us
  blocking collectives: 37.8 us -> 0 us
  Pallas kernels: 0 us -> 36.5 us
  starting transfers between devices: 10.5 us -> 0 us
  local copies, waits for them, and re-layouts: 0.78 us -> 7.02 us
  waiting for transfers between devices: 4.52 us -> 0 us
  other arithmetic: 1.21 us -> 0 us
    dot_general x14 -> x0, matrix products: 41.1 us -> none  [the longest x3 12.8 us: filter_along(): return jnp.einsum('ab,ijbf->ijaf', matrix, field_block, precision=HIGHEST)]
    psum x1 -> x0, blocking collectives: 37.8 us -> none  [body(): summed = lax.psum(density_part, 'grp')]
    pallas_call x0 -> x1, Pallas kernels: none -> 36.5 us  [fused_body(): pl.pallas_call(functools.partial(fused_kernel, groups, doms, cap), out_sh...]
    all_to_all x2 -> x0, starting transfers between devices: 8.52 us -> none  [the longest x1 5.16 us: body(): lax.all_to_all(outgoing, 'grp', split_axis=0, concat_axis=0, tiled=True)]
    unnamed x12 -> x14, local copies, waits for them, and re-layouts: 0.67 us -> 7.02 us
    all_to_all x2 -> x0, waiting for transfers between devices: 4.51 us -> none  [the longest x1 4.51 us: body(): lax.all_to_all(products, 'grp', split_axis=0, concat_axis=0, tiled=True)]
    ppermute x1 -> x0, starting transfers between devices: 2.03 us -> none  [passed_along(): return lax.ppermute(block, axis, route)]
  transfers between devices with their start and end apart: 3 -> 0, of which waited for: 1 -> 0; matrix products, arithmetic and copies ran while one was open for 4% -> 0% of each run, Pallas kernels for 0% -> 0%
where the time goes in v1:
time: 44.4 us; the launch traced here: 44.2 us
  Pallas kernels  36.5 us (82%)
  local copies, waits for them, and re-layouts  7.02 us (16%)
  between operations  0.65 us (1%)
    pallas_call x1, Pallas kernels, fused_body(): pl.pallas_call(functools.partial(fused_kernel, groups, doms, cap), out_sh...  36.5 us
    unnamed x14, local copies, waits for them, and re-layouts  7.02 us

profile of v1, /device:TPU:0, one launch (start us, length us, event | category | flops | bytes accessed | tf_op | source)
XLA Modules:
  0.0 44.2 jit_solution(11645664466234446536)
XLA Ops:
  0.6 0.0 copy-start
  0.6 1.6 %copy-done = f32[16,16,16,128]{3,2,1,0:T(8,128)S(1)} copy-done((f32[16,16,16,128]{3,2,1,0:T(8,128)S(1)}, f32[16,16,16,128]{3,2,1,0:T(8,128)}, u32[]{:S(2)}) %copy-start) | copy-done | bytes 2097176
  2.2 0.0 copy-start.1
  2.2 1.6 %copy-done.1 = f32[16,16,16,128]{3,2,1,0:T(8,128)S(1)} copy-done((f32[16,16,16,128]{3,2,1,0:T(8,128)S(1)}, f32[16,16,16,128]{3,2,1,0:T(8,128)}, u32[]{:S(2)}) %copy-start.1) | copy-done | bytes 2097176
  3.8 0.0 copy-start.2
  3.8 0.7 %copy-done.2 = f32[16]{0:T(128)S(1)} copy-done((f32[16]{0:T(128)S(1)}, f32[16]{0:T(128)}, u32[]{:S(2)}) %copy-start.2) | copy-done | bytes 88
  4.5 0.0 copy-start.3
  4.5 0.7 %copy-done.3 = f32[16]{0:T(128)S(1)} copy-done((f32[16]{0:T(128)S(1)}, f32[16]{0:T(128)}, u32[]{:S(2)}) %copy-start.3) | copy-done | bytes 88
  5.1 0.0 copy-start.4
  5.1 0.7 %copy-done.4 = s32[128,1]{0,1:T(1,128)S(1)} copy-done((s32[128,1]{0,1:T(1,128)S(1)}, s32[128,1]{0,1:T(1,128)}, u32[]{:S(2)}) %copy-start.4) | copy-done | bytes 536
  5.8 0.0 copy-start.5
  5.8 0.7 %copy-done.5 = f32[128]{0:T(128)S(1)} copy-done((f32[128]{0:T(128)S(1)}, f32[128]{0:T(128)}, u32[]{:S(2)}) %copy-start.5) | copy-done | bytes 536
  6.4 36.5 %shard_map.77 = (f32[128,128]{1,0:T(8,128)S(1)}, f32[8,256]{1,0:T(8,128)S(1)}) custom-call(f32[16]{0:T(128)S(1)} %copy-done.2, f32[16]{0:T(128)S(1)} %copy-done.3, s32[1,128]{1,0:T(1,128)S(1)} %bitcast.2, f32[1,128]{1,0:T(1,128)S(1)} %bitcast.3, f32[16,16,16,128]{3,2,1,0:T(8,128)S(1)} %copy-done, f32[16,16,16,128]{3,2,1,0:T(8,128)S(1)} %copy-done.1), custom_call_target="tpu_custom_call" | custom-call | tf_op jit(solution)/shard_map/pallas_call | solution.py:385
  42.9 0.6 %copy.10 = f32[128,128]{1,0:T(8,128)} copy(f32[128,128]{1,0:T(8,128)S(1)} %get-tuple-element.4) | data formatting | bytes 131072
  43.6 0.6 %copy.11 = f32[8,256]{1,0:T(8,128)} copy(f32[8,256]{1,0:T(8,128)S(1)} %get-tuple-element.5) | data formatting | bytes 16384
Async XLA Ops:
  0.6 1.6 %copy-start = (f32[16,16,16,128]{3,2,1,0:T(8,128)S(1)}, f32[16,16,16,128]{3,2,1,0:T(8,128)}, u32[]{:S(2)}) copy-start(f32[16,16,16,128]{3,2,1,0:T(8,128)} %support_ref.1) | copy-start | bytes 6291460
  2.2 1.6 %copy-start.1 = (f32[16,16,16,128]{3,2,1,0:T(8,128)S(1)}, f32[16,16,16,128]{3,2,1,0:T(8,128)}, u32[]{:S(2)}) copy-start(f32[16,16,16,128]{3,2,1,0:T(8,128)} %potential_ref.1) | copy-start | bytes 6291460
  3.8 0.7 %copy-start.2 = (f32[16]{0:T(128)S(1)}, f32[16]{0:T(128)}, u32[]{:S(2)}) copy-start(f32[16]{0:T(128)} %magic_ref.1) | copy-start | bytes 196
  4.5 0.7 %copy-start.3 = (f32[16]{0:T(128)S(1)}, f32[16]{0:T(128)}, u32[]{:S(2)}) copy-start(f32[16]{0:T(128)} %kinetic_ref.1) | copy-start | bytes 196
  5.1 0.7 %copy-start.4 = (s32[128,1]{0,1:T(1,128)S(1)}, s32[128,1]{0,1:T(1,128)}, u32[]{:S(2)}) copy-start(s32[128,1]{0,1:T(1,128)} %param.11) | copy-start | bytes 1540
  5.8 0.7 %copy-start.5 = (f32[128]{0:T(128)S(1)}, f32[128]{0:T(128)}, u32[]{:S(2)}) copy-start(f32[128]{0:T(128)} %param.10) | copy-start | bytes 1540

commit v2 on v1

--- a/solution.py
+++ b/solution.py
@@ -116,9 +116,9 @@
 
 def fused_kernel(
     groups, doms, cap,
-    magic_ref, kinetic_ref, owners_ref, kdiag_ref, support_ref, potential_ref,
-    margin_ref, density_ref,
-    x_ref, v_ref, y_ref, z_ref, xh_ref, xl_ref, w_ref, taps_ref, send_ref, recv_ref,
+    magic_hbm, kinetic_hbm, owners_hbm, kdiag_hbm, support_ref, potential_ref,
+    out_ref,
+    magic_ref, kinetic_ref, owners_ref, kdiag_ref, x_ref, v_ref, y_ref, z_ref, xh_ref, xl_ref, w_ref, taps_ref, send_ref, recv_ref,
     acc_ref, dens_ref, halo_ref, comb_ref, prod_ref, back_ref, disp_ref, disp_t_ref,
     load_sem, send_sem, recv_sem, bs_sem, br_sem, ds_sem, dr_sem, hs_sem, hr_sem,
 ):
@@ -132,15 +132,32 @@
     dom_next = lax.rem(dom + 1, doms)
     dom_prev = lax.rem(dom + doms - 1, doms)
 
-    load_x = pltpu.make_async_copy(support_ref, x_ref, load_sem.at[0])
-    load_v = pltpu.make_async_copy(potential_ref, v_ref, load_sem.at[1])
-    load_x.start()
-    load_v.start()
+    small = [
+        pltpu.make_async_copy(magic_hbm, magic_ref, load_sem.at[0]),
+        pltpu.make_async_copy(kinetic_hbm, kinetic_ref, load_sem.at[1]),
+        pltpu.make_async_copy(owners_hbm, owners_ref, load_sem.at[2]),
+        pltpu.make_async_copy(kdiag_hbm, kdiag_ref, load_sem.at[3]),
+    ]
+    part = side // 4
+    load_x, load_v = [
+        [
+            pltpu.make_async_copy(
+                source.at[pl.ds(part * n, part)], target.at[pl.ds(part * n, part)], load_sem.at[first + n]
+            )
+            for n in range(4)
+        ]
+        for source, target, first in ((support_ref, x_ref, 4), (potential_ref, v_ref, 8))
+    ]
+    for copy in small + load_x + load_v:
+        copy.start()
 
     barrier = pltpu.get_barrier_semaphore()
     for d in range(1, groups):
         pl.semaphore_signal(barrier, inc=1, device_id={"grp": lax.rem(me + d, groups)}, device_id_type=MESH)
     pl.semaphore_signal(barrier, inc=1, device_id={"dom": dom_prev}, device_id_type=MESH)
+
+    for copy in small:
+        copy.wait()
 
     for t in range(3 * side):
         taps_ref[t] = kinetic_ref[t - side] if side <= t < 2 * side else jnp.float32(0.0)
@@ -211,7 +228,8 @@
         second = ref[2 * n + 1].reshape(plane, funcs)
         return jnp.concatenate([first, second], axis=1)
 
-    load_x.wait()
+    for copy in load_x:
+        copy.wait()
 
     def stage_a(n, carry):
         high, low = split(pair_mid(x_ref, n))
@@ -222,8 +240,10 @@
         y_ref[:, 2 * n + 1] = out[:, funcs:].reshape(side, side, funcs)
         return carry
 
-    lax.fori_loop(0, chunks, stage_a, 0)
-    load_v.wait()
+    for n in range(chunks):
+        stage_a(n, 0)
+    for copy in load_v:
+        copy.wait()
 
     dens_row = lax.broadcasted_iota(jnp.int32, (side, 2 * funcs), 0)
     dens_half = lax.broadcasted_iota(jnp.int32, (side, 2 * funcs), 1) >> 7
@@ -240,7 +260,8 @@
         z_ref[2 * n + 1] = out[:, funcs:].reshape(side, side, funcs)
         return carry
 
-    lax.fori_loop(0, chunks, stage_b, 0)
+    for n in range(chunks):
+        stage_b(n, 0)
 
     pl.semaphore_wait(barrier, groups)
 
@@ -348,7 +369,7 @@
     total = comb_ref[0]
     for g in range(1, groups):
         total = total + comb_ref[g]
-    density_ref[...] = total
+    out_ref[:half] = total
 
     for d in order:
         get(d).wait_recv()
@@ -356,7 +377,8 @@
     if padded > slots:
         returned = jnp.concatenate([returned, jnp.zeros((padded - slots, funcs), F32)], axis=0)
     high, low = split(returned)
-    margin_ref[...] = mm(disp_t_ref[...], high) + mm(disp_t_ref[...], low)
+    out_ref[half:, :funcs] = mm(disp_t_ref[...], high) + mm(disp_t_ref[...], low)
+    out_ref[half:, funcs:] = jnp.zeros((funcs, plane - funcs), F32)
 
     def drain(n, carry):
         for d in order:
@@ -378,19 +400,19 @@
     chunks = side // 2
     padded = -(-groups * cap // 128) * 128
     vmem = pl.BlockSpec(memory_space=pltpu.VMEM)
-    smem = pl.BlockSpec(memory_space=pltpu.SMEM)
-    anywhere = pl.BlockSpec(memory_space=pl.ANY)
+    hbm = pl.BlockSpec(memory_space=pltpu.HBM)
     box = (side, side, side, funcs)
     dma = pltpu.SemaphoreType.DMA
-    margin, density = pl.pallas_call(
+    both = pl.pallas_call(
         functools.partial(fused_kernel, groups, doms, cap),
-        out_shape=(
-            jax.ShapeDtypeStruct((funcs, funcs), F32),
-            jax.ShapeDtypeStruct((side // 2, plane), F32),
-        ),
-        in_specs=[smem, smem, vmem, vmem, anywhere, anywhere],
-        out_specs=(vmem, vmem),
+        out_shape=jax.ShapeDtypeStruct((side // 2 + funcs, plane), F32),
+        in_specs=[hbm] * 6,
+        out_specs=vmem,
         scratch_shapes=[
+            pltpu.SMEM(magic_taps.shape, F32),
+            pltpu.SMEM(kinetic_taps.shape, F32),
+            pltpu.VMEM((1, funcs), jnp.int32),
+            pltpu.VMEM((1, funcs), F32),
             pltpu.VMEM(box, F32),
             pltpu.VMEM(box, F32),
             pltpu.VMEM(box, F32),
@@ -409,7 +431,7 @@
             pltpu.VMEM((groups, cap, funcs), F32),
             pltpu.VMEM((groups * cap, funcs), BF16),
             pltpu.VMEM((funcs, padded), BF16),
-            dma((2,)),
+            dma((12,)),
             dma((chunks, groups)),
             dma((chunks, groups)),
             dma((groups,)),
@@ -420,13 +442,13 @@
             dma,
         ],
         compiler_params=pltpu.CompilerParams(
-            collective_id=0, has_side_effects=True, vmem_limit_bytes=40 * 2**20
+            collective_id=0, has_side_effects=True, vmem_limit_bytes=63 * 2**20
         ),
     )(
         magic_taps, kinetic_taps, owners.reshape(1, funcs), kernel_diag.reshape(1, funcs),
         support, potential,
     )
-    return (margin, density)
+    return (both[side // 2:, :funcs], both[:side // 2])
 
 
 def body(doms, support, potential, magic_taps, kinetic_taps, kernel_diag, owners):

time: 44.4 us -> 36.7 us (0.83)
  local copies, waits for them, and re-layouts: 7.02 us -> 2.77 us
  Pallas kernels: 36.5 us -> 33.1 us
    unnamed x14 -> x0, local copies, waits for them, and re-layouts: 7.02 us -> none
    pallas_call x1, Pallas kernels: 36.5 us -> 33.1 us  [fused_body(): pl.pallas_call(functools.partial(fused_kernel, groups, doms, cap), out_sh...]
    slice x0 -> x2, local copies, waits for them, and re-layouts: none -> 2.77 us  [fused_body(): return (both[side // 2:, :funcs], both[:side // 2])]
where the time goes in v2:
time: 36.7 us; the launch traced here: 36.5 us
  Pallas kernels  33.1 us (90%)
  local copies, waits for them, and re-layouts  2.77 us (8%)
  between operations  0.64 us (2%)
    pallas_call x1, Pallas kernels, fused_body(): pl.pallas_call(functools.partial(fused_kernel, groups, doms, cap), out_sh...  33.1 us
    slice x2, local copies, waits for them, and re-layouts, fused_body(): return (both[side // 2:, :funcs], both[:side // 2])  2.77 us

profile of v2, /device:TPU:0, one launch (start us, length us, event | category | flops | bytes accessed | tf_op | source)
XLA Modules:
  0.0 36.5 jit_solution(3002316927051352522)
XLA Ops:
  0.6 33.1 %shard_map.77 = f32[136,256]{1,0:T(8,128)} custom-call(f32[16]{0:T(128)} %magic_hbm.1, f32[16]{0:T(128)} %kinetic_hbm.1, s32[1,128]{1,0:T(1,128)} %bitcast.2, f32[1,128]{1,0:T(1,128)} %bitcast.3, f32[16,16,16,128]{3,2,1,0:T(8,128)} %support_ref.1, f32[16,16,16,128]{3,2,1,0:T(8,128)} %potential_ref.1), custom_call_target="tpu_custom_call" | custom-call | tf_op jit(solution)/shard_map/pallas_call | solution.py:406
  33.7 1.3 %slice.7 = f32[8,256]{1,0:T(8,128)} slice(f32[136,256]{1,0:T(8,128)} %shard_map.77), slice={[0:8], [0:256]} | slice | bytes 16384 | tf_op jit(solution)/shard_map/slice | solution.py:451
  35.0 1.5 %slice.6 = f32[128,128]{1,0:T(8,128)} slice(f32[136,256]{1,0:T(8,128)} %shard_map.77), slice={[8:136], [0:128]} | slice | bytes 131072 | tf_op jit(solution)/shard_map/slice | solution.py:451

commit v3 on v2

--- a/solution.py
+++ b/solution.py
@@ -117,7 +117,7 @@
 def fused_kernel(
     groups, doms, cap,
     magic_hbm, kinetic_hbm, owners_hbm, kdiag_hbm, support_ref, potential_ref,
-    out_ref,
+    margin_ref, density_ref,
     magic_ref, kinetic_ref, owners_ref, kdiag_ref, x_ref, v_ref, y_ref, z_ref, xh_ref, xl_ref, w_ref, taps_ref, send_ref, recv_ref,
     acc_ref, dens_ref, halo_ref, comb_ref, prod_ref, back_ref, disp_ref, disp_t_ref,
     load_sem, send_sem, recv_sem, bs_sem, br_sem, ds_sem, dr_sem, hs_sem, hr_sem,
@@ -128,6 +128,7 @@
     chunks = side // 2
     slots = groups * cap
     me = lax.axis_index("grp")
+    core = lax.rem(me, 2)
     dom = lax.axis_index("dom")
     dom_next = lax.rem(dom + 1, doms)
     dom_prev = lax.rem(dom + doms - 1, doms)
@@ -193,10 +194,45 @@
         back_out * same_in,
         kin_out * same_in + same_out * kin_in,
     ]
-    for n, matrix in enumerate(matrices):
-        high, low = split(matrix)
+
+    def keep_matrix(n):
+        high, low = split(matrices[n])
         w_ref[2 * n] = high
         w_ref[2 * n + 1] = low
+
+    keep_matrix(0)
+
+    kdiag = kdiag_ref[...]
+    kdiag_pair = jnp.concatenate([kdiag, kdiag], axis=1) * (1.0 / float(funcs * groups))
+    dens_ref[...] = jnp.zeros_like(dens_ref)
+    acc_ref[...] = jnp.zeros_like(acc_ref)
+
+    def pair_mid(ref, n):
+        first = ref[:, 2 * n].reshape(plane, funcs)
+        second = ref[:, 2 * n + 1].reshape(plane, funcs)
+        return jnp.concatenate([first, second], axis=1)
+
+    def pair_top(ref, n):
+        first = ref[2 * n].reshape(plane, funcs)
+        second = ref[2 * n + 1].reshape(plane, funcs)
+        return jnp.concatenate([first, second], axis=1)
+
+    for copy in load_x:
+        copy.wait()
+
+    def stage_a(n, carry):
+        high, low = split(pair_mid(x_ref, n))
+        xh_ref[n] = high
+        xl_ref[n] = low
+        out = mm3(w_ref[0], w_ref[1], high, low).astype(BF16)
+        y_ref[:, 2 * n] = out[:, :funcs].reshape(side, side, funcs)
+        y_ref[:, 2 * n + 1] = out[:, funcs:].reshape(side, side, funcs)
+        return carry
+
+    for n in range(chunks):
+        stage_a(n, 0)
+        if 1 <= n < 5:
+            keep_matrix(n)
 
     owner = owners_ref[...]
     named = jnp.where(lax.broadcasted_iota(jnp.int32, (16, funcs), 0) == owner, 1.0, 0.0)
@@ -213,35 +249,6 @@
     disp_ref[...] = dispatch[:slots].astype(BF16)
     disp_t_ref[...] = dispatch.T.astype(BF16)
 
-    kdiag = kdiag_ref[...]
-    kdiag_pair = jnp.concatenate([kdiag, kdiag], axis=1) * (1.0 / float(funcs * groups))
-    dens_ref[...] = jnp.zeros_like(dens_ref)
-    acc_ref[...] = jnp.zeros_like(acc_ref)
-
-    def pair_mid(ref, n):
-        first = ref[:, 2 * n].reshape(plane, funcs)
-        second = ref[:, 2 * n + 1].reshape(plane, funcs)
-        return jnp.concatenate([first, second], axis=1)
-
-    def pair_top(ref, n):
-        first = ref[2 * n].reshape(plane, funcs)
-        second = ref[2 * n + 1].reshape(plane, funcs)
-        return jnp.concatenate([first, second], axis=1)
-
-    for copy in load_x:
-        copy.wait()
-
-    def stage_a(n, carry):
-        high, low = split(pair_mid(x_ref, n))
-        xh_ref[n] = high
-        xl_ref[n] = low
-        out = mm3(w_ref[0], w_ref[1], high, low)
-        y_ref[:, 2 * n] = out[:, :funcs].reshape(side, side, funcs)
-        y_ref[:, 2 * n + 1] = out[:, funcs:].reshape(side, side, funcs)
-        return carry
-
-    for n in range(chunks):
-        stage_a(n, 0)
     for copy in load_v:
         copy.wait()
 
@@ -249,13 +256,13 @@
     dens_half = lax.broadcasted_iota(jnp.int32, (side, 2 * funcs), 1) >> 7
 
     def stage_b(n, carry):
-        high, low = split(pair_top(y_ref, n))
-        real = mm3(w_ref[2], w_ref[3], high, low)
+        block = pair_top(y_ref, n)
+        real = mm(w_ref[2], block) + mm(w_ref[3], block)
         squared = (real * real * kdiag_pair).astype(BF16)
         chosen = jnp.where(dens_row == dens_half + 2 * n, 1.0, 0.0).astype(BF16)
         dens_ref[...] += lax.dot_general(chosen, squared, NT, preferred_element_type=F32)
-        high, low = split(pair_top(v_ref, n) * real)
-        out = mm3(w_ref[4], w_ref[5], high, low)
+        block = (pair_top(v_ref, n) * real).astype(BF16)
+        out = mm(w_ref[4], block) + mm(w_ref[5], block)
         z_ref[2 * n] = out[:, :funcs].reshape(side, side, funcs)
         z_ref[2 * n + 1] = out[:, funcs:].reshape(side, side, funcs)
         return carry
@@ -272,10 +279,20 @@
     )
     halo.start()
 
-    order = [1 + (groups // 2 + n) % (groups - 1) for n in range(groups - 1)]
+    order = range(1, groups)
+
+    def partner(d):
+        far, near = me // 4, lax.rem(me // 2, 2)
+        return (
+            lax.rem(far + d // 4, 2) * 4 + lax.rem(near + lax.rem(d // 2, 2), 2) * 2
+            + lax.rem(core + lax.rem(d, 2), 2)
+        )
+
+    even, odd = (6, 2, 4, 7, 3, 5, 1), (4, 6, 2, 5, 7, 3, 1)
+    sequence = [jnp.int32(a) + core * jnp.int32(b - a) for a, b in zip(even, odd)]
 
     def bulk(n, d):
-        peer = lax.rem(me + d, groups)
+        peer = partner(d)
         return pltpu.make_async_remote_copy(
             src_ref=send_ref.at[n, peer], dst_ref=recv_ref.at[n, me],
             send_sem=send_sem.at[n, d], recv_sem=recv_sem.at[n, d],
@@ -283,7 +300,7 @@
         )
 
     def arrived(n, d):
-        source = lax.rem(me + groups - d, groups)
+        source = partner(d)
         return pltpu.make_async_remote_copy(
             src_ref=send_ref.at[n, source], dst_ref=recv_ref.at[n, source],
             send_sem=send_sem.at[n, d], recv_sem=recv_sem.at[n, d],
@@ -305,7 +322,7 @@
             send_ref[n, o] = jnp.concatenate(
                 [rows[0][o * cap:(o + 1) * cap], rows[1][o * cap:(o + 1) * cap]], axis=0
             ).astype(BF16)
-        for d in order:
+        for d in sequence:
             bulk(n, d).start()
         recv_ref[n, me] = send_ref[n, me]
         return carry
@@ -316,14 +333,14 @@
     comb_ref[me] = dens_ref[:half] + halo_ref[...]
 
     def spread(d, source):
-        peer = lax.rem(me + d, groups)
+        peer = partner(d)
         return pltpu.make_async_remote_copy(
             src_ref=comb_ref.at[source], dst_ref=comb_ref.at[source],
             send_sem=ds_sem.at[d], recv_sem=dr_sem.at[d],
             device_id={"grp": peer}, device_id_type=MESH,
         )
 
-    for d in order:
+    for d in sequence:
         spread(d, me).start()
 
     lax.fori_loop(chunks // 2, chunks, stage_c, 0)
@@ -345,7 +362,7 @@
         )
 
     def give(d):
-        peer = lax.rem(me + d, groups)
+        peer = partner(d)
         return pltpu.make_async_remote_copy(
             src_ref=prod_ref.at[peer], dst_ref=back_ref.at[me],
             send_sem=bs_sem.at[d], recv_sem=br_sem.at[d],
@@ -353,23 +370,23 @@
         )
 
     def get(d):
-        source = lax.rem(me + groups - d, groups)
+        source = partner(d)
         return pltpu.make_async_remote_copy(
             src_ref=prod_ref.at[source], dst_ref=back_ref.at[source],
             send_sem=bs_sem.at[d], recv_sem=br_sem.at[d],
             device_id={"grp": source}, device_id_type=MESH,
         )
 
-    for d in order:
+    for d in sequence:
         give(d).start()
     back_ref[me] = prod_ref[me]
 
     for d in order:
-        spread(d, lax.rem(me + groups - d, groups)).wait_recv()
+        spread(d, partner(d)).wait_recv()
     total = comb_ref[0]
     for g in range(1, groups):
         total = total + comb_ref[g]
-    out_ref[:half] = total
+    density_ref[...] = total
 
     for d in order:
         get(d).wait_recv()
@@ -377,8 +394,7 @@
     if padded > slots:
         returned = jnp.concatenate([returned, jnp.zeros((padded - slots, funcs), F32)], axis=0)
     high, low = split(returned)
-    out_ref[half:, :funcs] = mm(disp_t_ref[...], high) + mm(disp_t_ref[...], low)
-    out_ref[half:, funcs:] = jnp.zeros((funcs, plane - funcs), F32)
+    margin_ref[...] = mm(disp_t_ref[...], high) + mm(disp_t_ref[...], low)
 
     def drain(n, carry):
         for d in order:
@@ -403,11 +419,14 @@
     hbm = pl.BlockSpec(memory_space=pltpu.HBM)
     box = (side, side, side, funcs)
     dma = pltpu.SemaphoreType.DMA
-    both = pl.pallas_call(
+    return pl.pallas_call(
         functools.partial(fused_kernel, groups, doms, cap),
-        out_shape=jax.ShapeDtypeStruct((side // 2 + funcs, plane), F32),
+        out_shape=(
+            jax.ShapeDtypeStruct((funcs, funcs), F32),
+            jax.ShapeDtypeStruct((side // 2, plane), F32),
+        ),
         in_specs=[hbm] * 6,
-        out_specs=vmem,
+        out_specs=(vmem, vmem),
         scratch_shapes=[
             pltpu.SMEM(magic_taps.shape, F32),
             pltpu.SMEM(kinetic_taps.shape, F32),
@@ -415,7 +434,7 @@
             pltpu.VMEM((1, funcs), F32),
             pltpu.VMEM(box, F32),
             pltpu.VMEM(box, F32),
-            pltpu.VMEM(box, F32),
+            pltpu.VMEM(box, BF16),
             pltpu.VMEM(box, F32),
             pltpu.VMEM((chunks, plane, 2 * funcs), BF16),
             pltpu.VMEM((chunks, plane, 2 * funcs), BF16),
@@ -448,7 +467,6 @@
         magic_taps, kinetic_taps, owners.reshape(1, funcs), kernel_diag.reshape(1, funcs),
         support, potential,
     )
-    return (both[side // 2:, :funcs], both[:side // 2])
 
 
 def body(doms, support, potential, magic_taps, kinetic_taps, kernel_diag, owners):
@@ -456,7 +474,7 @@
     funcs = support.shape[3]
     groups = lax.axis_size("grp")
     cap = max(2, 3 * funcs // (2 * groups))
-    fits = side == 16 and magic_taps.shape[0] == 16 and funcs == 128 and groups <= 8
+    fits = side == 16 and magic_taps.shape[0] == 16 and funcs == 128 and groups == 8
     if fits and cap % 8 == 0 and doms > 1:
         return fused_body(doms, support, potential, magic_taps, kinetic_taps, kernel_diag, owners)
     return general_body(support, potential, magic_taps, kinetic_taps, kernel_diag, owners)

time: 36.7 us -> 36.7 us (level)
    slice x2 -> x0, local copies, waits for them, and re-layouts: 2.77 us -> none  [fused_body(): return (both[side // 2:, :funcs], both[:side // 2])]
    unnamed x0 -> x2, local copies, waits for them, and re-layouts: none -> 2.77 us
where the time goes in v3:
time: 36.7 us; the launch traced here: 36.5 us
  Pallas kernels  33 us (90%)
  local copies, waits for them, and re-layouts  2.77 us (8%)
  between operations  0.64 us (2%)
    pallas_call x1, Pallas kernels, fused_body(): pl.pallas_call(functools.partial(fused_kernel, groups, doms, cap), out_sh...  33 us
    unnamed x2, local copies, waits for them, and re-layouts  2.77 us

profile of v3, /device:TPU:0, one launch (start us, length us, event | category | flops | bytes accessed | tf_op | source)
XLA Modules:
  0.0 36.5 jit_solution(8781168429335464428)
XLA Ops:
  0.6 33.0 %shard_map.77 = (f32[128,128]{1,0:T(8,128)}, f32[8,256]{1,0:T(8,128)}) custom-call(f32[16]{0:T(128)} %magic_hbm.1, f32[16]{0:T(128)} %kinetic_hbm.1, s32[1,128]{1,0:T(1,128)} %bitcast.2, f32[1,128]{1,0:T(1,128)} %bitcast.3, f32[16,16,16,128]{3,2,1,0:T(8,128)} %support_ref.1, f32[16,16,16,128]{3,2,1,0:T(8,128)} %potential_ref.1), custom_call_target="tpu_custom_call" | custom-call | tf_op jit(solution)/shard_map/pallas_call | solution.py:422
  33.7 1.5 %copy.10 = f32[128,128]{1,0:T(8,128)} copy(f32[128,128]{1,0:T(8,128)} %get-tuple-element.4) | data formatting | bytes 131072
  35.2 1.3 %copy.11 = f32[8,256]{1,0:T(8,128)} copy(f32[8,256]{1,0:T(8,128)} %get-tuple-element.5) | data formatting | bytes 16384

commit v4 on v3

--- a/solution.py
+++ b/solution.py
@@ -119,7 +119,7 @@
     magic_hbm, kinetic_hbm, owners_hbm, kdiag_hbm, support_ref, potential_ref,
     margin_ref, density_ref,
     magic_ref, kinetic_ref, owners_ref, kdiag_ref, x_ref, v_ref, y_ref, z_ref, xh_ref, xl_ref, w_ref, taps_ref, send_ref, recv_ref,
-    acc_ref, dens_ref, halo_ref, comb_ref, prod_ref, back_ref, disp_ref, disp_t_ref,
+    acc_ref, dens_ref, halo_ref, comb_ref, prod_ref, back_ref, disp_ref, disp_t_ref, cells_ref,
     load_sem, send_sem, recv_sem, bs_sem, br_sem, ds_sem, dr_sem, hs_sem, hr_sem,
 ):
     side = x_ref.shape[0]
@@ -204,7 +204,7 @@
 
     kdiag = kdiag_ref[...]
     kdiag_pair = jnp.concatenate([kdiag, kdiag], axis=1) * (1.0 / float(funcs * groups))
-    dens_ref[...] = jnp.zeros_like(dens_ref)
+    cells_ref[...] = jnp.zeros_like(cells_ref)
     acc_ref[...] = jnp.zeros_like(acc_ref)
 
     def pair_mid(ref, n):
@@ -252,15 +252,15 @@
     for copy in load_v:
         copy.wait()
 
-    dens_row = lax.broadcasted_iota(jnp.int32, (side, 2 * funcs), 0)
-    dens_half = lax.broadcasted_iota(jnp.int32, (side, 2 * funcs), 1) >> 7
+    dens_lane = lax.broadcasted_iota(jnp.int32, (2 * funcs, funcs), 1)
+    dens_half = lax.broadcasted_iota(jnp.int32, (2 * funcs, funcs), 0) >> 7
 
     def stage_b(n, carry):
         block = pair_top(y_ref, n)
         real = mm(w_ref[2], block) + mm(w_ref[3], block)
         squared = (real * real * kdiag_pair).astype(BF16)
-        chosen = jnp.where(dens_row == dens_half + 2 * n, 1.0, 0.0).astype(BF16)
-        dens_ref[...] += lax.dot_general(chosen, squared, NT, preferred_element_type=F32)
+        chosen = jnp.where(dens_lane == dens_half + 2 * n, 1.0, 0.0).astype(BF16)
+        cells_ref[...] += mm(squared, chosen)
         block = (pair_top(v_ref, n) * real).astype(BF16)
         out = mm(w_ref[4], block) + mm(w_ref[5], block)
         z_ref[2 * n] = out[:, :funcs].reshape(side, side, funcs)
@@ -269,6 +269,8 @@
 
     for n in range(chunks):
         stage_b(n, 0)
+
+    dens_ref[...] = cells_ref[...].T[:side]
 
     pl.semaphore_wait(barrier, groups)
 
@@ -307,7 +309,7 @@
             device_id={"grp": source}, device_id_type=MESH,
         )
 
-    def stage_c(n, carry):
+    def chunk_rows(n):
         zh, zl = split(pair_mid(z_ref, n))
         grad = mm3(w_ref[6], w_ref[7], zh, zl) + mm3(w_ref[8], w_ref[9], xh_ref[n], xl_ref[n])
         rows = []
@@ -318,16 +320,30 @@
                 along = along + taps_ref[other - j + (side // 2 - 1 + side)] * x_ref[:, other]
             block = (grad[:, p * funcs:(p + 1) * funcs] + along.reshape(plane, funcs)).astype(BF16)
             rows.append(lax.dot_general(disp_ref[...], block, NT, preferred_element_type=F32))
-        for o in range(groups):
-            send_ref[n, o] = jnp.concatenate(
+        return [
+            jnp.concatenate(
                 [rows[0][o * cap:(o + 1) * cap], rows[1][o * cap:(o + 1) * cap]], axis=0
             ).astype(BF16)
-        for d in sequence:
-            bulk(n, d).start()
-        recv_ref[n, me] = send_ref[n, me]
+            for o in range(groups)
+        ]
+
+    def stage_c(numbers):
+        made = [chunk_rows(n) for n in numbers]
+        for n, blocks in zip(numbers, made):
+            for o in range(groups):
+                send_ref[n, o] = blocks[o]
+        for n in numbers:
+            for d in sequence:
+                bulk(n, d).start()
+        for n in numbers:
+            recv_ref[n, me] = send_ref[n, me]
+
+    def two_chunks(m, carry):
+        stage_c((2 * m + 1, 2 * m + 2))
         return carry
 
-    lax.fori_loop(0, chunks // 2, stage_c, 0)
+    stage_c((0,))
+    lax.fori_loop(0, chunks // 4, two_chunks, 0)
 
     halo.wait()
     comb_ref[me] = dens_ref[:half] + halo_ref[...]
@@ -343,7 +359,8 @@
     for d in sequence:
         spread(d, me).start()
 
-    lax.fori_loop(chunks // 2, chunks, stage_c, 0)
+    lax.fori_loop(chunks // 4, chunks // 2 - 1, two_chunks, 0)
+    stage_c((chunks - 1,))
 
     def stage_d(n, carry):
         for d in order:
@@ -405,6 +422,17 @@
     for d in order:
         spread(d, me).wait_send()
         give(d).wait_send()
+
+
+def deliver_kernel(margin_ref, density_ref, margin_out, density_out, sem):
+    copies = [
+        pltpu.make_async_copy(margin_ref, margin_out, sem.at[0]),
+        pltpu.make_async_copy(density_ref, density_out, sem.at[1]),
+    ]
+    for copy in copies:
+        copy.start()
+    for copy in copies:
+        copy.wait()
 
 
 def fused_body(doms, support, potential, magic_taps, kinetic_taps, kernel_diag, owners):
@@ -419,7 +447,7 @@
     hbm = pl.BlockSpec(memory_space=pltpu.HBM)
     box = (side, side, side, funcs)
     dma = pltpu.SemaphoreType.DMA
-    return pl.pallas_call(
+    margin, density = pl.pallas_call(
         functools.partial(fused_kernel, groups, doms, cap),
         out_shape=(
             jax.ShapeDtypeStruct((funcs, funcs), F32),
@@ -450,6 +478,7 @@
             pltpu.VMEM((groups, cap, funcs), F32),
             pltpu.VMEM((groups * cap, funcs), BF16),
             pltpu.VMEM((funcs, padded), BF16),
+            pltpu.VMEM((plane, funcs), F32),
             dma((12,)),
             dma((chunks, groups)),
             dma((chunks, groups)),
@@ -467,6 +496,17 @@
         magic_taps, kinetic_taps, owners.reshape(1, funcs), kernel_diag.reshape(1, funcs),
         support, potential,
     )
+    return pl.pallas_call(
+        deliver_kernel,
+        out_shape=(
+            jax.ShapeDtypeStruct(margin.shape, F32),
+            jax.ShapeDtypeStruct(density.shape, F32),
+        ),
+        in_specs=[hbm, hbm],
+        out_specs=(hbm, hbm),
+        scratch_shapes=[dma((2,))],
+        compiler_params=pltpu.CompilerParams(vmem_limit_bytes=63 * 2**20),
+    )(margin, density)
 
 
 def body(doms, support, potential, magic_taps, kinetic_taps, kernel_diag, owners):

time: 36.7 us -> 37.1 us (1.011)
  Pallas kernels: 33 us -> 36.3 us
  local copies, waits for them, and re-layouts: 2.77 us -> 0 us
    pallas_call x0 -> x1, Pallas kernels: none -> 3.35 us  [fused_body(): pl.pallas_call(deliver_kernel, out_shape=(jax.ShapeDtypeStruct(margin.sha...]
    unnamed x2 -> x0, local copies, waits for them, and re-layouts: 2.77 us -> none
where the time goes in v4:
time: 37.1 us; the launch traced here: 36.9 us
  Pallas kernels  36.3 us (98%)
  between operations  0.64 us (2%)
    pallas_call x1, Pallas kernels, fused_body(): pl.pallas_call(functools.partial(fused_kernel, groups, doms, cap), out_sh...  33 us
    pallas_call x1, Pallas kernels, fused_body(): pl.pallas_call(deliver_kernel, out_shape=(jax.ShapeDtypeStruct(margin.sha...  3.35 us

profile of v4, /device:TPU:0, one launch (start us, length us, event | category | flops | bytes accessed | tf_op | source)
XLA Modules:
  0.0 36.9 jit_solution(13818140877533801973)
XLA Ops:
  0.6 33.0 %shard_map.77 = (f32[128,128]{1,0:T(8,128)}, f32[8,256]{1,0:T(8,128)}) custom-call(f32[16]{0:T(128)} %magic_hbm.1, f32[16]{0:T(128)} %kinetic_hbm.1, s32[1,128]{1,0:T(1,128)} %bitcast.2, f32[1,128]{1,0:T(1,128)} %bitcast.3, f32[16,16,16,128]{3,2,1,0:T(8,128)} %support_ref.1, f32[16,16,16,128]{3,2,1,0:T(8,128)} %potential_ref.1), custom_call_target="tpu_custom_call" | custom-call | tf_op jit(solution)/shard_map/pallas_call | solution.py:450
  33.6 3.4 %shard_map.78 = (f32[128,128]{1,0:T(8,128)}, f32[8,256]{1,0:T(8,128)}) custom-call(f32[128,128]{1,0:T(8,128)} %get-tuple-element.4.margin_ref, f32[8,256]{1,0:T(8,128)} %get-tuple-element.5.density_ref), custom_call_target="tpu_custom_call" | custom-call | tf_op jit(solution)/shard_map/pallas_call | solution.py:499

commit v5 on v4

--- a/solution.py
+++ b/solution.py
@@ -424,17 +424,6 @@
         give(d).wait_send()
 
 
-def deliver_kernel(margin_ref, density_ref, margin_out, density_out, sem):
-    copies = [
-        pltpu.make_async_copy(margin_ref, margin_out, sem.at[0]),
-        pltpu.make_async_copy(density_ref, density_out, sem.at[1]),
-    ]
-    for copy in copies:
-        copy.start()
-    for copy in copies:
-        copy.wait()
-
-
 def fused_body(doms, support, potential, magic_taps, kinetic_taps, kernel_diag, owners):
     side = support.shape[0]
     funcs = support.shape[3]
@@ -450,8 +439,8 @@
     margin, density = pl.pallas_call(
         functools.partial(fused_kernel, groups, doms, cap),
         out_shape=(
-            jax.ShapeDtypeStruct((funcs, funcs), F32),
-            jax.ShapeDtypeStruct((side // 2, plane), F32),
+            pltpu.VMEM((funcs, funcs), F32),
+            pltpu.VMEM((side // 2, plane), F32),
         ),
         in_specs=[hbm] * 6,
         out_specs=(vmem, vmem),
@@ -496,17 +485,7 @@
         magic_taps, kinetic_taps, owners.reshape(1, funcs), kernel_diag.reshape(1, funcs),
         support, potential,
     )
-    return pl.pallas_call(
-        deliver_kernel,
-        out_shape=(
-            jax.ShapeDtypeStruct(margin.shape, F32),
-            jax.ShapeDtypeStruct(density.shape, F32),
-        ),
-        in_specs=[hbm, hbm],
-        out_specs=(hbm, hbm),
-        scratch_shapes=[dma((2,))],
-        compiler_params=pltpu.CompilerParams(vmem_limit_bytes=63 * 2**20),
-    )(margin, density)
+    return (margin, density)
 
 
 def body(doms, support, potential, magic_taps, kinetic_taps, kernel_diag, owners):

time: 37.1 us -> 34.3 us (0.925)
  Pallas kernels: 36.3 us -> 32.3 us
  local copies, waits for them, and re-layouts: 0 us -> 1.23 us
    pallas_call x1 -> x0, Pallas kernels: 3.35 us -> none  [fused_body(): pl.pallas_call(deliver_kernel, out_shape=(jax.ShapeDtypeStruct(margin.sha...]
    unnamed x0 -> x2, local copies, waits for them, and re-layouts: none -> 1.23 us
    pallas_call x1, Pallas kernels: 33 us -> 32.3 us  [fused_body(): pl.pallas_call(functools.partial(fused_kernel, groups, doms, cap), out_sh...]
where the time goes in v5:
time: 34.3 us; the launch traced here: 34.2 us
  Pallas kernels  32.3 us (94%)
  local copies, waits for them, and re-layouts  1.23 us (4%)
  between operations  0.64 us (2%)
    pallas_call x1, Pallas kernels, fused_body(): pl.pallas_call(functools.partial(fused_kernel, groups, doms, cap), out_sh...  32.3 us
    unnamed x2, local copies, waits for them, and re-layouts  1.23 us

profile of v5, /device:TPU:0, one launch (start us, length us, event | category | flops | bytes accessed | tf_op | source)
XLA Modules:
  0.0 34.2 jit_solution(13079662817970537604)
XLA Ops:
  0.6 32.3 %shard_map.77 = (f32[128,128]{1,0:T(8,128)S(1)}, f32[8,256]{1,0:T(8,128)S(1)}) custom-call(f32[16]{0:T(128)} %magic_hbm.1, f32[16]{0:T(128)} %kinetic_hbm.1, s32[1,128]{1,0:T(1,128)} %bitcast.2, f32[1,128]{1,0:T(1,128)} %bitcast.3, f32[16,16,16,128]{3,2,1,0:T(8,128)} %support_ref.1, f32[16,16,16,128]{3,2,1,0:T(8,128)} %potential_ref.1), custom_call_target="tpu_custom_call" | custom-call | tf_op jit(solution)/shard_map/pallas_call | solution.py:439
  33.0 0.6 %copy.10 = f32[128,128]{1,0:T(8,128)} copy(f32[128,128]{1,0:T(8,128)S(1)} %get-tuple-element.2) | data formatting | bytes 131072
  33.6 0.6 %copy.11 = f32[8,256]{1,0:T(8,128)} copy(f32[8,256]{1,0:T(8,128)S(1)} %get-tuple-element.3) | data formatting | bytes 16384
